TPU v7x, 512 devices: a whole 4x8x8 slice. The times are simulated.
512 devices in a mesh: dp: 32 (over x, y), row: 4 (over z_hi, core), col: 4 (over z_lo).
Axes of the slice: x: 4, y: 8, z: 8 (z_hi: 2, z_lo: 4; z = z_hi * 4 + z_lo), core: 2. Of those that a mesh axis runs over, the one named last changes fastest.
Arguments:
- grad_out: bfloat16 [32768, 8192], P('dp', ('col', 'row')), may hold values from -6 to 6
- weight: bfloat16 [28672, 8192], P(('dp', 'row'), 'col'), may hold values from -6 to 6
Outputs:
- gram: float32 [1024, 8192], P(('dp', 'row'), 'col')
- product: float32 [28672, 1024], P(('dp', 'row'), 'col')
All inputs are finite; a program needn't handle non-finite values.
Results may differ from a plain program's by a relative error of at most 0.0029.
Values may be sent and summed in bfloat16 or wider, within the bound.
A program may use at most 64 MiB of HBM per device.

v0:
```python
import jax
import jax.numpy as jnp
from jax import lax
from jax.sharding import PartitionSpec as P

WIN_BLK = 64
TOK_DP = 1024


def apply_rows(weight, rows):
    return lax.dot_general(
        weight, rows, (((1,), (1,)), ((), ())), preferred_element_type=jnp.float32
    )


def shards(grad_out, weight):
    n_dp = lax.axis_size("dp")
    total = TOK_DP * n_dp
    own_window = grad_out[:, :WIN_BLK]
    window = lax.all_gather(own_window, "col", axis=1, tiled=True)
    tile = (
        jnp.dot(
            window.T,
            lax.all_gather(grad_out, "row", axis=1, tiled=True),
            preferred_element_type=jnp.float32,
        )
        / total
    )
    gram = lax.psum_scatter(tile, "dp", scatter_dimension=0, tiled=True)
    partial_product = apply_rows(
        weight, lax.all_gather(gram.astype(jnp.bfloat16), ("dp", "row"), axis=0, tiled=True)
    )
    product = lax.psum_scatter(partial_product, "col", scatter_dimension=1, tiled=True)
    return (gram, product)


def solution(mesh):
    placed = (P("dp", ("col", "row")), P(("dp", "row"), "col"))
    return jax.shard_map(
        shards,
        mesh=mesh,
        in_specs=placed,
        out_specs=(P(("dp", "row"), "col"), P(("dp", "row"), "col")),
        check_vma=False,
    )
```

profile of v0, /device:TPU:1, one launch (start us, length us, event | category | flops | bytes accessed | tf_op | source)
XLA Modules:
  0.0 490.5 jit_solution(14473768966431216381)
XLA Ops:
  7.2 0.0 copy-start
  7.2 0.0 all-gather.3.cloned.1.call-start
  7.2 0.7 all-gather.3.cloned.1.call-update
  7.9 0.0 reduce-scatter.3.cloned.1.call-start
  8.0 1.0 slice.3
  8.9 0.1 copy.5
  9.1 17.7 %all_gather.9 = bf16[1024,256]{0,1:T(8,128)(2,1)S(1)} all-gather(bf16[1024,64]{0,1:T(8,128)(2,1)S(1)} %copy.5), channel_id=1, replica_groups=mesh['dp'=32,'row'=4,'col'=4] {'col'}, dimensions={1}, use_global_device_ids=true | all-gather | bytes 655360 | tf_op jit(solution)/shard_map/all_gather | solution.py:20
  26.8 58.9 %all-gather.3.cloned.1.call-done = bf16[1024,2048]{1,0:T(8,128)(2,1)} async-done(((bf16[1024,512]{1,0:T(8,128)(2,1)}), bf16[1024,2048]{1,0:T(8,128)(2,1)}) %all-gather.3.cloned.1.call-update) | async-done | bytes 4194320 | tf_op jit(solution)/shard_map/all_gather | solution.py:24
  85.7 4.8 convolution_multiply_fusion
  90.5 0.0 reduce-scatter.3.cloned.1.call-update
  90.5 0.0 all-gather.5.cloned.1.call-start
  90.5 212.6 %reduce-scatter.3.cloned.1.call-done = f32[8,2048]{1,0:T(8,128)} async-done(((f32[256,2048]{1,0:T(8,128)}), f32[8,2048]{1,0:T(8,128)}) %reduce-scatter.3.cloned.1.call-update) | async-done | bytes 65552 | tf_op jit(solution)/shard_map/reduce_scatter | solution.py:29
  303.1 1.5 convert_element_type.3
  304.6 0.0 all-gather.5.cloned.1.call-update
  304.6 0.0 reduce-scatter.5.cloned.1.call-start
  304.6 148.4 %all-gather.5.cloned.1.call-done = bf16[1024,2048]{1,0:T(8,128)(2,1)} async-done(((bf16[8,2048]{1,0:T(8,128)(2,1)}), bf16[1024,2048]{1,0:T(8,128)(2,1)}) %all-gather.5.cloned.1.call-update) | async-done | bytes 4194320 | tf_op jit(solution)/shard_map/all_gather | solution.py:31
  453.0 0.0 copy-done
  453.0 4.5 convolution_bitcast_fusion
  457.5 0.0 reduce-scatter.5.cloned.1.call-update
  457.5 26.4 %reduce-scatter.5.cloned.1.call-done = f32[224,256]{1,0:T(8,128)} async-done(((f32[224,1024]{1,0:T(8,128)}), f32[224,256]{1,0:T(8,128)}) %reduce-scatter.5.cloned.1.call-update) | async-done | bytes 229392 | tf_op jit(solution)/shard_map/reduce_scatter | solution.py:33
Async XLA Ops:
  7.2 445.8 %copy-start = (bf16[224,2048]{1,0:T(8,128)(2,1)S(1)}, bf16[224,2048]{1,0:T(8,128)(2,1)}, u32[]{:S(2)}) copy-start(bf16[224,2048]{1,0:T(8,128)(2,1)} %param.3) | copy-start | bytes 2752516
  7.2 78.5 %all-gather.3.cloned.1.call-start = ((), (), s32[]{:S(2)}) async-start(), calls=%async_computation.2 | async-start | bytes 5242880 | tf_op jit(solution)/shard_map/all_gather | solution.py:24
  7.9 295.2 %reduce-scatter.3.cloned.1.call-start = ((), (), s32[]{:S(2)}) async-start(), calls=%async_computation.3 | async-start | bytes 2162688 | tf_op jit(solution)/shard_map/reduce_scatter | solution.py:29
  90.5 362.5 %all-gather.5.cloned.1.call-start = ((), (), s32[]{:S(2)}) async-start(), calls=%async_computation.4 | async-start | bytes 4227072 | tf_op jit(solution)/shard_map/all_gather | solution.py:31
  304.6 179.4 %reduce-scatter.5.cloned.1.call-start = ((), (), s32[]{:S(2)}) async-start(), calls=%async_computation.5 | async-start | bytes 1146880 | tf_op jit(solution)/shard_map/reduce_scatter | solution.py:33
Sparse Core Ops, SparseCore 0:
  10.1 75.5 all-gather.2
  90.7 212.3 reduce-scatter.2
  309.1 143.8 all-gather.4
  457.6 26.2 reduce-scatter.4
where the time goes:
time: 491 us; the launch traced here: 490 us
  waiting for transfers between devices  447 us (91%)
  blocking collectives  17.7 us (4%)
  between operations  13.8 us (3%)
  matrix products  9.29 us (2%)
    reduce_scatter x1, waiting for transfers between devices, shards(): gram = lax.psum_scatter(tile, 'dp', scatter_dimension=0, tiled=True)  213 us
    all_gather x1, waiting for transfers between devices, shards(): lax.all_gather(gram.astype(jnp.bfloat16), ('dp', 'row'), axis=0, tiled=True)  148 us
    all_gather x1, waiting for transfers between devices, shards(): lax.all_gather(grad_out, 'row', axis=1, tiled=True)  58.9 us
    reduce_scatter x1, waiting for transfers between devices, shards(): lax.psum_scatter(partial_product, 'col', scatter_dimension=1, tiled=True)  26.4 us
    all_gather x1, blocking collectives, shards(): window = lax.all_gather(own_window, 'col', axis=1, tiled=True)  17.7 us
  transfers between devices with their start and end apart: 4, of which 4 were waited for; matrix products, arithmetic and copies ran while one was open for 0% of the time, Pallas kernels for 0%

commit v1 on v0

v1 whole, which is shorter than its diff:
```python
import functools

import jax
import jax.numpy as jnp
from jax import lax
from jax.experimental import pallas as pl
from jax.experimental.pallas import tpu as pltpu
from jax.sharding import PartitionSpec as P

MESH = pl.DeviceIdType.MESH
F32, BF16 = jnp.float32, jnp.bfloat16
TOTAL = 32768
X_TYPE, Y_TYPE, Z_TYPE = BF16, F32, F32


def kernel(
    g_hbm, w_hbm, gram_ref, prod_ref,
    g, wt, part, own, x_in, s, y_in, t, gram_in, low, w, gl, q, z_in,
    load_sem, ring_send, ring_recv, sib_send, sib_recv, w_send, w_recv,
    x_send, x_recv, y_send, y_recv, h_send, h_recv, low_send, low_recv,
    ay_send, ay_recv, ax_send, ax_recv, z_send, z_recv,
):
    dp, row, c = lax.axis_index("dp"), lax.axis_index("row"), lax.axis_index("col")
    x, y, h, k = dp // 8, dp % 8, row // 2, row % 2
    z = h * 4 + c
    mate = 1 - k

    def at(px, py, pz, pk):
        return (px * 8 + py, (pz // 4) * 2 + pk, pz % 4)

    def copy(src, dst, send, recv, device):
        return pltpu.make_async_remote_copy(
            src_ref=src, dst_ref=dst, send_sem=send, recv_sem=recv,
            device_id=device, device_id_type=MESH,
        )

    sibling = at(x, y, z, mate)

    def arrived(dst, recv):
        copy(dst, dst, recv, recv, sibling).wait_recv()

    def sent(src, send):
        copy(src, src, send, send, sibling).wait_send()

    load_g = pltpu.make_async_copy(g_hbm, g, load_sem.at[0])
    load_w = pltpu.make_async_copy(w_hbm, w.at[k], load_sem.at[1])
    load_g.start()
    load_w.start()

    barrier = pltpu.get_barrier_semaphore()
    partners = [sibling]
    partners += [at((x + i) % 4, y, z, k) for i in range(1, 4)]
    for pk in range(2):
        partners += [at(x, (y + i) % 8, z, pk) for i in range(1, 8)]
        partners += [at(x, y, (z + i) % 8, pk) for i in range(1, 8)]
    for partner in partners:
        pl.semaphore_signal(barrier, inc=1, device_id=partner, device_id_type=MESH)

    def slot(pz, pk):
        return (pz % 4) * 4 + (pz // 4) * 2 + pk

    def half(b, j):
        return wt.at[b, pl.ds(32 * j, 32)]

    load_g.wait()
    mine = slot(z, k)
    wt[mine] = g[:, :128].astype(F32).T[:64].astype(BF16)
    load_w.wait()
    pl.semaphore_wait(barrier, len(partners))

    up, down = at(x, y, (z + 1) % 8, k), at(x, y, (z + 7) % 8, k)
    to = (up, down)

    def ring(direction, b, step, j):
        return copy(
            half(b, j), half(b, j), ring_send.at[direction, step, j],
            ring_recv.at[direction, step, j], to[direction],
        )

    def share(b, step, j):
        return copy(half(b, j), half(b, j), sib_send.at[step, j], sib_recv.at[step, j], sibling)

    for j in range(2):
        ring(0, mine, 0, j).start()
        ring(1, mine, 0, j).start()
    for j in range(2):
        share(mine, 0, j).start()
    w_copy = copy(w.at[k], w.at[k], w_send, w_recv, sibling)
    w_copy.start()
    for step in range(1, 4):
        for j in range(2):
            for direction in range(2):
                away = step if direction == 1 else 8 - step
                b = slot((z + away) % 8, k)
                arrived(half(b, j), ring_recv.at[direction, step - 1, j])
                if step < 3 or direction == j:
                    ring(direction, b, step, j).start()
                share(b, away, j).start()
    far = slot((z + 4) % 8, k)
    for j in range(2):
        arrived(half(far, j), ring_recv.at[j, 3, j])
        share(far, 4, j).start()
    for step in range(8):
        for j in range(2):
            arrived(half(slot((z + step) % 8, mate), j), sib_recv.at[step, j])

    def rows_of(px):
        left = wt[pl.ds(px * 4, 4)].reshape(256, 1024)
        got = jnp.dot(left, g[...], preferred_element_type=F32)
        return jnp.concatenate(
            [got[64 * r + 8 * i : 64 * r + 8 * i + 8] for i in range(8) for r in range(4)], axis=0
        )

    for n, away in enumerate((2, 1, 3)):
        px = (x + away) % 4
        part[n] = rows_of(px).astype(X_TYPE)
        copy(part.at[n], x_in.at[away - 1], x_send.at[away - 1], x_recv.at[away - 1], at(px, y, z, k)).start()
    own[...] = rows_of(x)
    for away in (1, 3, 2):
        arrived(x_in.at[away - 1], x_recv.at[away - 1])
    for i in range(8):
        rows = pl.ds(32 * i, 32)
        s[i] = own[rows] + x_in[0, rows].astype(F32) + x_in[1, rows].astype(F32) + x_in[2, rows].astype(F32)

    for away in (4, 3, 5, 2, 6, 1, 7):
        py = (y + away) % 8
        copy(s.at[py], y_in.at[away - 1], y_send.at[away - 1], y_recv.at[away - 1], at(x, py, z, k)).start()
    total = s[y]
    for away in (1, 7, 2, 6, 3, 5, 4):
        arrived(y_in.at[away - 1], y_recv.at[away - 1])
        total += y_in[away - 1]
    total = total * (1.0 / TOTAL)

    low[h] = total.astype(BF16)
    t[...] = total
    partner_low = copy(low.at[h], low.at[h], low_send, low_recv, at(x, y, (z + 4) % 8, k))
    partner_low.start()
    for away in range(1, 4):
        pr = (row + away) % 4
        copy(
            t.at[pl.ds(pl.multiple_of(8 * pr, 8), 8)], gram_in.at[row],
            h_send.at[away - 1], h_recv.at[away - 1], (dp, pr, c),
        ).start()
    gram_in[row] = t[pl.ds(pl.multiple_of(8 * row, 8), 8)]

    keeper = x // 2
    xi = x % 2

    def spread(ph, n):
        for away in (4, 3, 5, 2, 6, 1, 7):
            copy(
                low.at[ph], gl.at[xi, 2 * ph + k, y], ay_send.at[n, away],
                ay_recv.at[ph, k, away], at(x, (y + away) % 8, z, keeper),
            ).start()

        @pl.when(k == keeper)
        def _():
            gl[xi, 2 * ph + k, y] = low[ph]

        @pl.when(k != keeper)
        def _():
            copy(
                low.at[ph], gl.at[xi, 2 * ph + k, y], ay_send.at[n, 0], ay_recv.at[ph, k, 0], sibling
            ).start()

    spread(h, 0)
    arrived(low.at[1 - h], low_recv)
    spread(1 - h, 1)

    right, left = at((x + 1) % 4, y, z, k), at((x + 3) % 4, y, z, k)

    def pass_on(i, hk, n, device):
        return copy(gl.at[i, hk], gl.at[i, hk], ax_send.at[n], ax_recv.at[i, hk], device)

    def gather_own():
        for ph in (h, 1 - h):
            for pk in range(2):
                for away in range(8):
                    block = gl.at[xi, 2 * ph + pk, (y + 8 - away) % 8]
                    if away:
                        arrived(block, ay_recv.at[ph, pk, away])
                    else:

                        @pl.when(pk != k)
                        def _():
                            arrived(block, ay_recv.at[ph, pk, 0])

                pass_on(xi, 2 * ph + pk, 4 * pk + 2 * ph, right).start()
                pass_on(xi, 2 * ph + pk, 4 * pk + 2 * ph + 1, left).start()

    def gather_near(i, pk, device):
        for ph in (h, 1 - h):
            for which in range(2):
                arrived(gl.at[i, 2 * ph + which], ax_recv.at[i, 2 * ph + which])
                if which == pk:
                    pass_on(i, 2 * ph + which, 8 + ph, device).start()

    def gather_far(i):
        for hk in range(4):
            arrived(gl.at[i, hk], ax_recv.at[i, hk])

    def multiply(i):
        px = 2 * k + i
        for pk in range(2):
            acc = jnp.zeros((224, 256), F32)
            for hk in range(4):
                acc += lax.dot_general(
                    w[pk, :, 512 * hk : 512 * hk + 512], gl[i, hk].reshape(256, 512),
                    (((1,), (1,)), ((), ())), preferred_element_type=F32,
                )
            q[i, pk] = acc.astype(Z_TYPE)
            here = (c == px) & (k == pk)

            @pl.when(here)
            def _():
                z_in[c] = q[i, pk]

            @pl.when(jnp.logical_not(here))
            def _():
                copy(
                    q.at[i, pk], z_in.at[c], z_send.at[i, pk], z_recv.at[c], at(x, y, h * 4 + px, pk)
                ).start()

    sent(w.at[k], w_send)
    arrived(w.at[mate], w_recv)

    def near(i):
        rel = (2 * k + i - x + 4) % 4

        @pl.when(rel == 1)
        def _():
            gather_near(i, 1, left)

        @pl.when(rel == 3)
        def _():
            gather_near(i, 0, right)

    @pl.when(k == keeper)
    def _():
        gather_own()
        multiply(xi)
        near(1 - xi)
        multiply(1 - xi)

    @pl.when(k != keeper)
    def _():
        close = 1 - xi
        near(close)
        multiply(close)
        gather_far(1 - close)
        multiply(1 - close)

    for away in range(1, 4):
        pr = (row + 4 - away) % 4
        arrived(gram_in.at[pr], h_recv.at[away - 1])
    for r in range(4):
        gram_ref[:, 512 * r : 512 * r + 512] = gram_in[r]

    for away in range(4):
        pc = (c + away) % 4
        if away:
            arrived(z_in.at[pc], z_recv.at[pc])
        else:

            @pl.when(k != c // 2)
            def _():
                arrived(z_in.at[c], z_recv.at[c])

    prod_ref[...] = (
        z_in[0].astype(F32) + z_in[1].astype(F32) + z_in[2].astype(F32) + z_in[3].astype(F32)
    )

    for j in range(2):
        for direction in range(2):
            for step in range(3):
                sent(half(mine, j), ring_send.at[direction, step, j])
        sent(half(mine, j), ring_send.at[j, 3, j])
        for step in range(8):
            sent(half(mine, j), sib_send.at[step, j])
    for n in range(3):
        sent(part.at[n], x_send.at[n])
    for n in range(7):
        sent(s.at[0], y_send.at[n])
    sent(low.at[h], low_send)
    for n in range(3):
        sent(gram_in.at[0], h_send.at[n])
    for n in range(2):
        for away in range(1, 8):
            sent(low.at[0], ay_send.at[n, away])

        @pl.when(k != keeper)
        def _():
            sent(low.at[0], ay_send.at[n, 0])

    @pl.when(k == keeper)
    def _():
        for n in range(8):
            sent(gl.at[0, 0], ax_send.at[n])

    for n in range(2):
        sent(gl.at[0, 0], ax_send.at[8 + n])
    for i in range(2):
        for pk in range(2):
            here = (c == 2 * k + i) & (k == pk)

            @pl.when(jnp.logical_not(here))
            def _():
                sent(q.at[i, pk], z_send.at[i, pk])


def shards(grad_out, weight):
    dma = pltpu.SemaphoreType.DMA
    return pl.pallas_call(
        kernel,
        name="curvature",
        out_shape=(
            jax.ShapeDtypeStruct((8, 2048), F32),
            jax.ShapeDtypeStruct((224, 256), F32),
        ),
        in_specs=[pl.BlockSpec(memory_space=pl.ANY)] * 2,
        out_specs=(pl.BlockSpec(memory_space=pltpu.VMEM),) * 2,
        scratch_shapes=[
            pltpu.VMEM((1024, 512), BF16),
            pltpu.VMEM((16, 64, 1024), BF16),
            pltpu.VMEM((3, 256, 512), X_TYPE),
            pltpu.VMEM((256, 512), F32),
            pltpu.VMEM((3, 256, 512), X_TYPE),
            pltpu.VMEM((8, 32, 512), Y_TYPE),
            pltpu.VMEM((7, 32, 512), Y_TYPE),
            pltpu.VMEM((32, 512), F32),
            pltpu.VMEM((4, 8, 512), F32),
            pltpu.VMEM((2, 32, 512), BF16),
            pltpu.VMEM((2, 224, 2048), BF16),
            pltpu.VMEM((2, 4, 8, 32, 512), BF16),
            pltpu.VMEM((2, 2, 224, 256), Z_TYPE),
            pltpu.VMEM((4, 224, 256), Z_TYPE),
            dma((2,)),
            dma((2, 4, 2)), dma((2, 4, 2)),
            dma((8, 2)), dma((8, 2)),
            dma, dma,
            dma((3,)), dma((3,)),
            dma((7,)), dma((7,)),
            dma((3,)), dma((3,)),
            dma, dma,
            dma((2, 8)), dma((2, 2, 8)),
            dma((10,)), dma((2, 4)),
            dma((2, 2)), dma((4,)),
        ],
        compiler_params=pltpu.CompilerParams(
            collective_id=0, has_side_effects=True, vmem_limit_bytes=48 * 2**20
        ),
        cost_estimate=pl.CostEstimate(flops=2 * 10**9, bytes_accessed=3 * 2**20, transcendentals=0),
    )(grad_out, weight)


def solution(mesh):
    placed = (P("dp", ("col", "row")), P(("dp", "row"), "col"))
    return jax.shard_map(
        shards,
        mesh=mesh,
        in_specs=placed,
        out_specs=(P(("dp", "row"), "col"), P(("dp", "row"), "col")),
        check_vma=False,
    )
```

time: 491 us -> 114 us (0.23)
  the two profiles are of different devices: /device:TPU:1 before, /device:TPU:5 now
where the time goes in v1:
time: 114 us
  Pallas kernels  110 us (96%)
  local copies, waits for them, and re-layouts  3.72 us (3%)
    pallas_call x1, Pallas kernels, shards(): pl.pallas_call(kernel, name='curvature', out_shape=(jax.ShapeDtypeStruct(...  110 us
    unnamed x6, local copies, waits for them, and re-layouts  3.72 us

profile of v1, /device:TPU:5, one launch (start us, length us, event | category | flops | bytes accessed | tf_op | source)
XLA Modules:
  0.0 114.3 jit_solution(10352749261234698370)
XLA Ops:
  0.6 0.0 copy-start
  0.6 1.2 %copy-done = bf16[1024,512]{1,0:T(8,128)(2,1)S(1)} copy-done((bf16[1024,512]{1,0:T(8,128)(2,1)S(1)}, bf16[1024,512]{1,0:T(8,128)(2,1)}, u32[]{:S(2)}) %copy-start) | copy-done | bytes 1048600
  1.9 0.0 copy-start.1
  1.9 1.2 %copy-done.1 = bf16[224,2048]{1,0:T(8,128)(2,1)S(1)} copy-done((bf16[224,2048]{1,0:T(8,128)(2,1)S(1)}, bf16[224,2048]{1,0:T(8,128)(2,1)}, u32[]{:S(2)}) %copy-start.1) | copy-done | bytes 917528
  3.0 109.9 %curvature.1 = (f32[8,2048]{1,0:T(8,128)S(1)}, f32[224,256]{1,0:T(8,128)S(1)}) custom-call(bf16[1024,512]{1,0:T(8,128)(2,1)S(1)} %copy-done, bf16[224,2048]{1,0:T(8,128)(2,1)S(1)} %copy-done.1), custom_call_target="tpu_custom_call" | custom-call | flops 2000000000 | bytes 3145728 | tf_op jit(solution)/shard_map/curvature/pallas_call | solution.py:313
  113.0 0.6 copy.6
  113.6 0.7 copy.7
Async XLA Ops:
  0.6 1.2 %copy-start = (bf16[1024,512]{1,0:T(8,128)(2,1)S(1)}, bf16[1024,512]{1,0:T(8,128)(2,1)}, u32[]{:S(2)}) copy-start(bf16[1024,512]{1,0:T(8,128)(2,1)} %g_hbm.1) | copy-start | bytes 3145732
  1.9 1.2 %copy-start.1 = (bf16[224,2048]{1,0:T(8,128)(2,1)S(1)}, bf16[224,2048]{1,0:T(8,128)(2,1)}, u32[]{:S(2)}) copy-start(bf16[224,2048]{1,0:T(8,128)(2,1)} %w_hbm.1) | copy-start | bytes 2752516

commit v2 on v0

v2 whole, which is shorter than its diff:
```python
import jax
import jax.numpy as jnp
from jax import lax
from jax.experimental import pallas as pl
from jax.experimental.pallas import tpu as pltpu
from jax.sharding import PartitionSpec as P

MESH = pl.DeviceIdType.MESH
F32, BF16 = jnp.float32, jnp.bfloat16
TOTAL = 32768
CH = 4
CW = 256
NQ = 4


def kernel(
    g_hbm, w_hbm, gram_ref, prod_ref,
    g, wt, pf, part, own, x_in, s, y_in, t, gram_in, low, w, gl, q, z_in,
    load_sem, swap_send, swap_recv, ring_send, ring_recv,
    x_send, x_recv, y_send, y_recv, h_send, h_recv, low_send, low_recv,
    ay_send, ay_recv, ax_send, ax_recv, fw_send, z_send, z_recv,
):
    dp, row, c = lax.axis_index("dp"), lax.axis_index("row"), lax.axis_index("col")
    x, y, h, k = dp // 8, dp % 8, row // 2, row % 2
    z = h * 4 + c

    def at(px, py, pz, pk):
        return (px * 8 + py, (pz // 4) * 2 + pk, pz % 4)

    def copy(src, dst, send, recv, device):
        return pltpu.make_async_remote_copy(
            src_ref=src, dst_ref=dst, send_sem=send, recv_sem=recv,
            device_id=device, device_id_type=MESH,
        )

    sibling = at(x, y, z, 1 - k)
    opposite = at(x, y, (z + 4) % 8, k)
    right, left = at((x + 1) % 4, y, z, k), at((x + 3) % 4, y, z, k)

    def arrived(dst, recv):
        copy(dst, dst, recv, recv, sibling).wait_recv()

    def sent(src, send):
        copy(src, src, send, send, sibling).wait_send()

    load_g = pltpu.make_async_copy(g_hbm, g.at[k], load_sem.at[0])
    load_w = pltpu.make_async_copy(w_hbm, w.at[k], load_sem.at[1])
    load_g.start()
    load_w.start()

    barrier = pltpu.get_barrier_semaphore()
    partners = [sibling]
    partners += [at((x + i) % 4, y, z, k) for i in range(1, 4)]
    partners += [at(x, (y + i) % 8, z, k) for i in range(1, 8)]
    partners += [at(x, y, (z + i) % 8, k) for i in range(1, 8)]
    partners += [at(x, y, h * 4 + (c + i) % 4, 1 - k) for i in range(1, 4)]
    for partner in partners:
        pl.semaphore_signal(barrier, inc=1, device_id=partner, device_id_type=MESH)

    def slot(pz):
        return (pz % 4) * 2 + pz // 4

    def piece(b, j):
        return wt.at[b, pl.ds(16 * j, 16)]

    load_g.wait()
    mine = slot(z)
    wt[mine] = g[k, :, :128].astype(F32).T[:64].astype(BF16)
    load_w.wait()
    pl.semaphore_wait(barrier, len(partners))

    to = (at(x, y, (z + 1) % 8, k), at(x, y, (z + 7) % 8, k))

    def ring(direction, b, step, j):
        return copy(
            piece(b, j), piece(b, j), ring_send.at[direction, step, j],
            ring_recv.at[direction, step, j], to[direction],
        )

    for j in range(NQ):
        ring(0, mine, 0, j).start()
        ring(1, mine, 0, j).start()
    copy(g.at[k], g.at[k], swap_send.at[0], swap_recv.at[0], sibling).start()
    copy(w.at[k], w.at[k], swap_send.at[1], swap_recv.at[1], sibling).start()
    for step in range(1, 4):
        for j in range(NQ):
            for direction in range(2):
                away = step if direction == 1 else 8 - step
                b = slot((z + away) % 8)
                arrived(piece(b, j), ring_recv.at[direction, step - 1, j])
                if step < 3 or direction == j // (NQ // 2):
                    ring(direction, b, step, j).start()
    far = slot((z + 4) % 8)
    for j in range(NQ):
        arrived(piece(far, j), ring_recv.at[j // (NQ // 2), 3, j])
    arrived(g.at[1 - k], swap_recv.at[0])

    def form(n):
        got = jnp.dot(
            wt[...].reshape(512, 1024), g[n // 2, :, CW * (n % 2) : CW * (n % 2) + CW],
            preferred_element_type=F32,
        )
        for px in range(4):
            for py in range(8):
                for ph in range(2):
                    a = 128 * px + 64 * ph + 8 * py
                    b = 16 * py + 8 * ph
                    pf[px, b : b + 8] = got[a : a + 8]
        for away in (2, 1, 3):
            px = (x + away) % 4
            part[n, away - 1] = pf[px].astype(BF16)
            copy(
                part.at[n, away - 1], x_in.at[n, away - 1],
                x_send.at[n, away - 1], x_recv.at[n, away - 1], at(px, y, z, k),
            ).start()
        own[n] = pf[x]

    def sum_x(n):
        for away in (1, 3, 2):
            arrived(x_in.at[n, away - 1], x_recv.at[n, away - 1])
        terms = x_in[n, 0].astype(F32) + x_in[n, 1].astype(F32) + x_in[n, 2].astype(F32)
        s[n] = (own[n] + terms).reshape(8, 16, CW)
        for away in (4, 3, 5, 2, 6, 1, 7):
            copy(
                s.at[n, (y + away) % 8], y_in.at[n, away - 1],
                y_send.at[n, away - 1], y_recv.at[n, away - 1], at(x, (y + away) % 8, z, k),
            ).start()

    def spread(ph, n):
        for away in (4, 3, 5, 2, 6, 1, 7):
            copy(
                low.at[ph, n], gl.at[x, ph, n, y], ay_send.at[ph, n, away - 1],
                ay_recv.at[ph, n, away - 1], at(x, (y + away) % 8, z, k),
            ).start()
        gl[x, ph, n, y] = low[ph, n]

    def sum_y(n):
        total = s[n, y]
        for away in (1, 7, 2, 6, 3, 5, 4):
            arrived(y_in.at[n, away - 1], y_recv.at[n, away - 1])
            total += y_in[n, away - 1]
        total = total * (1.0 / TOTAL)
        low[h, n] = total.astype(BF16)
        copy(low.at[h, n], low.at[h, n], low_send.at[n], low_recv.at[n], opposite).start()
        spread(h, n)
        t[n] = total
        copy(
            t.at[n, pl.ds(pl.multiple_of(8 * (1 - h), 8), 8)], gram_in.at[h, n],
            h_send.at[n], h_recv.at[n], opposite,
        ).start()
        gram_in[h, n] = t[n, pl.ds(pl.multiple_of(8 * h, 8), 8)]

    def spread_other(n):
        arrived(low.at[1 - h, n], low_recv.at[n])
        spread(1 - h, n)

    def pass_on(px, ph, n, send, recv, device):
        return copy(gl.at[px, ph, n], gl.at[px, ph, n], send, recv, device)

    def send_own(ph, n):
        for away in (1, 7, 2, 6, 3, 5, 4):
            arrived(gl.at[x, ph, n, (y + 8 - away) % 8], ay_recv.at[ph, n, away - 1])
        pass_on(x, ph, n, ax_send.at[0, ph, n], ax_recv.at[0, ph, n], right).start()
        pass_on(x, ph, n, ax_send.at[1, ph, n], ax_recv.at[1, ph, n], left).start()

    def send_near(ph, n):
        arrived(gl.at[(x + 3) % 4, ph, n], ax_recv.at[0, ph, n])
        if n < CH // 2:
            pass_on((x + 3) % 4, ph, n, fw_send.at[ph, n], ax_recv.at[2, ph, n], right).start()
        arrived(gl.at[(x + 1) % 4, ph, n], ax_recv.at[1, ph, n])
        if n >= CH // 2:
            pass_on((x + 1) % 4, ph, n, fw_send.at[ph, n], ax_recv.at[2, ph, n], left).start()

    def run(stage, n):
        if 0 <= n < CH:
            stage(n)

    for n in range(CH):
        form(n)
    for n in range(CH + 4):
        run(sum_x, n)
        run(sum_y, n - 1)
        run(lambda m: send_own(h, m), n - 2)
        run(spread_other, n - 2)
        run(lambda m: send_own(1 - h, m), n - 3)
        run(lambda m: send_near(h, m), n - 3)
        run(lambda m: send_near(1 - h, m), n - 4)

    def multiply(away):
        px = (x + away) % 4
        acc = jnp.zeros((448, 128), F32)
        for ph in range(2):
            for n in range(CH):
                a = 1024 * ph + CW * n
                acc += lax.dot_general(
                    w[:, :, a : a + CW].reshape(448, CW), gl[px, ph, n].reshape(128, CW),
                    (((1,), (1,)), ((), ())), preferred_element_type=F32,
                )
        q[away] = acc.astype(BF16).reshape(2, 224, 128)
        for pk in range(2):
            here = (c == px) & (k == pk)

            @pl.when(here)
            def _():
                z_in[c, k] = q[away, pk]

            @pl.when(jnp.logical_not(here))
            def _():
                copy(
                    q.at[away, pk], z_in.at[c, k], z_send.at[away, pk], z_recv.at[c, k],
                    at(x, y, h * 4 + px, pk),
                ).start()

    arrived(w.at[1 - k], swap_recv.at[1])
    multiply(0)
    multiply(1)
    multiply(3)
    for ph in range(2):
        for n in range(CH):
            arrived(gl.at[(x + 2) % 4, ph, n], ax_recv.at[2, ph, n])
    multiply(2)

    for n in range(CH):
        arrived(gram_in.at[1 - h, n], h_recv.at[n])
    for ph in range(2):
        for n in range(CH):
            a = 1024 * ph + CW * n
            gram_ref[:, a : a + CW] = gram_in[ph, n]

    for away in range(1, 4):
        for pk in range(2):
            pc = (c + away) % 4
            arrived(z_in.at[pc, pk], z_recv.at[pc, pk])
    arrived(z_in.at[c, 1 - k], z_recv.at[c, 1 - k])
    acc = jnp.zeros((224, 256), F32)
    source = lax.broadcasted_iota(jnp.int32, (128, 256), 0)
    target = lax.broadcasted_iota(jnp.int32, (128, 256), 1)
    for pk in range(2):
        place = (target == (source // 8) * 16 + 8 * pk + source % 8).astype(F32).astype(BF16)
        for pc in range(4):
            acc += jnp.dot(z_in[pc, pk], place, preferred_element_type=F32)
    prod_ref[...] = acc

    for j in range(NQ):
        for direction in range(2):
            for step in range(3):
                sent(piece(mine, j), ring_send.at[direction, step, j])
        sent(piece(mine, j), ring_send.at[j // (NQ // 2), 3, j])
    sent(g.at[k], swap_send.at[0])
    sent(w.at[k], swap_send.at[1])
    for n in range(CH):
        for away in range(3):
            sent(part.at[n, away], x_send.at[n, away])
        for away in range(7):
            sent(s.at[n, 0], y_send.at[n, away])
        sent(low.at[h, n], low_send.at[n])
        sent(gram_in.at[0, n], h_send.at[n])
        for ph in range(2):
            for away in range(7):
                sent(low.at[ph, n], ay_send.at[ph, n, away])
            for side in range(2):
                sent(gl.at[x, ph, n], ax_send.at[side, ph, n])
            sent(gl.at[x, ph, n], fw_send.at[ph, n])
    for away in range(4):
        for pk in range(2):

            @pl.when(jnp.logical_not((c == (x + away) % 4) & (k == pk)))
            def _():
                sent(q.at[away, pk], z_send.at[away, pk])


def shards(grad_out, weight):
    dma = pltpu.SemaphoreType.DMA
    return pl.pallas_call(
        kernel,
        name="curvature",
        out_shape=(
            jax.ShapeDtypeStruct((8, 2048), F32),
            jax.ShapeDtypeStruct((224, 256), F32),
        ),
        in_specs=[pl.BlockSpec(memory_space=pltpu.HBM)] * 2,
        out_specs=(pl.BlockSpec(memory_space=pltpu.VMEM),) * 2,
        scratch_shapes=[
            pltpu.VMEM((2, 1024, 512), BF16),
            pltpu.VMEM((8, 64, 1024), BF16),
            pltpu.VMEM((4, 128, CW), F32),
            pltpu.VMEM((CH, 3, 128, CW), BF16),
            pltpu.VMEM((CH, 128, CW), F32),
            pltpu.VMEM((CH, 3, 128, CW), BF16),
            pltpu.VMEM((CH, 8, 16, CW), F32),
            pltpu.VMEM((CH, 7, 16, CW), F32),
            pltpu.VMEM((CH, 16, CW), F32),
            pltpu.VMEM((2, CH, 8, CW), F32),
            pltpu.VMEM((2, CH, 16, CW), BF16),
            pltpu.VMEM((2, 224, 2048), BF16),
            pltpu.VMEM((4, 2, CH, 8, 16, CW), BF16),
            pltpu.VMEM((4, 2, 224, 128), BF16),
            pltpu.VMEM((4, 2, 224, 128), BF16),
            dma((2,)),
            dma((2,)), dma((2,)),
            dma((2, 4, NQ)), dma((2, 4, NQ)),
            dma((CH, 3)), dma((CH, 3)),
            dma((CH, 7)), dma((CH, 7)),
            dma((CH,)), dma((CH,)),
            dma((CH,)), dma((CH,)),
            dma((2, CH, 7)), dma((2, CH, 7)),
            dma((2, 2, CH)), dma((3, 2, CH)), dma((2, CH)),
            dma((4, 2)), dma((4, 2)),
        ],
        compiler_params=pltpu.CompilerParams(
            collective_id=0, has_side_effects=True, vmem_limit_bytes=48 * 2**20
        ),
        cost_estimate=pl.CostEstimate(flops=2 * 10**9, bytes_accessed=3 * 2**20, transcendentals=0),
    )(grad_out, weight)


def solution(mesh):
    placed = (P("dp", ("col", "row")), P(("dp", "row"), "col"))
    return jax.shard_map(
        shards,
        mesh=mesh,
        in_specs=placed,
        out_specs=(P(("dp", "row"), "col"), P(("dp", "row"), "col")),
        check_vma=False,
    )
```

time: 491 us -> 85.1 us (0.17)
  the two profiles are of different devices: /device:TPU:1 before, /device:TPU:5 now
where the time goes in v2:
time: 85.1 us; the launch traced here: 84.9 us
  Pallas kernels  80.5 us (95%)
  local copies, waits for them, and re-layouts  3.72 us (4%)
    pallas_call x1, Pallas kernels, shards(): pl.pallas_call(kernel, name='curvature', out_shape=(jax.ShapeDtypeStruct(...  80.5 us
    unnamed x6, local copies, waits for them, and re-layouts  3.72 us

profile of v2, /device:TPU:5, one launch (start us, length us, event | category | flops | bytes accessed | tf_op | source)
XLA Modules:
  0.0 84.9 jit_solution(15696053577112946142)
XLA Ops:
  0.6 0.0 copy-start
  0.6 1.2 %copy-done = bf16[1024,512]{1,0:T(8,128)(2,1)S(1)} copy-done((bf16[1024,512]{1,0:T(8,128)(2,1)S(1)}, bf16[1024,512]{1,0:T(8,128)(2,1)}, u32[]{:S(2)}) %copy-start) | copy-done | bytes 1048600
  1.9 0.0 copy-start.1
  1.9 1.2 %copy-done.1 = bf16[224,2048]{1,0:T(8,128)(2,1)S(1)} copy-done((bf16[224,2048]{1,0:T(8,128)(2,1)S(1)}, bf16[224,2048]{1,0:T(8,128)(2,1)}, u32[]{:S(2)}) %copy-start.1) | copy-done | bytes 917528
  3.0 80.5 %curvature.1 = (f32[8,2048]{1,0:T(8,128)S(1)}, f32[224,256]{1,0:T(8,128)S(1)}) custom-call(bf16[1024,512]{1,0:T(8,128)(2,1)S(1)} %copy-done, bf16[224,2048]{1,0:T(8,128)(2,1)S(1)} %copy-done.1), custom_call_target="tpu_custom_call" | custom-call | flops 2000000000 | bytes 3145728 | tf_op jit(solution)/shard_map/curvature/pallas_call | solution.py:274
  83.6 0.6 copy.6
  84.2 0.7 copy.7
Async XLA Ops:
  0.6 1.2 %copy-start = (bf16[1024,512]{1,0:T(8,128)(2,1)S(1)}, bf16[1024,512]{1,0:T(8,128)(2,1)}, u32[]{:S(2)}) copy-start(bf16[1024,512]{1,0:T(8,128)(2,1)} %g_hbm.1) | copy-start | bytes 3145732
  1.9 1.2 %copy-start.1 = (bf16[224,2048]{1,0:T(8,128)(2,1)S(1)}, bf16[224,2048]{1,0:T(8,128)(2,1)}, u32[]{:S(2)}) copy-start(bf16[224,2048]{1,0:T(8,128)(2,1)} %w_hbm.1) | copy-start | bytes 2752516

commit v3 on v2

v3 whole, which is shorter than its diff:
```python
import jax
import jax.numpy as jnp
from jax import lax
from jax.experimental import pallas as pl
from jax.experimental.pallas import tpu as pltpu
from jax.sharding import PartitionSpec as P

MESH = pl.DeviceIdType.MESH
F32, BF16 = jnp.float32, jnp.bfloat16
TOTAL = 32768
CH = 4
CW = 1024 // CH
U = 256 // CW
NQ = 4
LAG_Y, LAG_OWN, LAG_H, LAG_OWN2, LAG_NEAR, LAG_NEAR2, LAG_FAR, LAG_FAR2 = 1, 2, 2, 3, 3, 4, 4, 5


def kernel(
    g_hbm, w_hbm, gram_ref, prod_ref,
    win, g, wt, place, pf, part, own, x_in, s, y_in, t, gram_in, low, w, gl, acc, q, z_in,
    load_sem, swap_send, swap_recv, ring_send, ring_recv,
    x_send, x_recv, y_send, y_recv, h_send, h_recv, low_send, low_recv,
    ay_send, ay_recv, ax_send, ax_recv, fw_send, z_send, z_recv,
):
    dp, row, c = lax.axis_index("dp"), lax.axis_index("row"), lax.axis_index("col")
    x, y, h, k = dp // 8, dp % 8, row // 2, row % 2
    z = h * 4 + c

    xs = [x] + [(x + i) % 4 for i in range(1, 4)]
    ys = [y] + [(y + i) % 8 for i in range(1, 8)]

    def at(px, py, pz, pk):
        return (px * 8 + py, (pz // 4) * 2 + pk, pz % 4)

    def copy(src, dst, send, recv, device):
        return pltpu.make_async_remote_copy(
            src_ref=src, dst_ref=dst, send_sem=send, recv_sem=recv,
            device_id=device, device_id_type=MESH,
        )

    sibling = at(x, y, z, 1 - k)
    opposite = at(x, y, (z + 4) % 8, k)
    right, left = at(xs[1], y, z, k), at(xs[3], y, z, k)

    def arrived(dst, recv):
        copy(dst, dst, recv, recv, sibling).wait_recv()

    def sent(src, send):
        copy(src, src, send, send, sibling).wait_send()

    load_g = pltpu.make_async_copy(g_hbm, g.at[k], load_sem.at[0])
    load_w = pltpu.make_async_copy(w_hbm, w.at[k], load_sem.at[1])
    load_win = pltpu.make_async_copy(g_hbm.at[:, pl.ds(0, 128)], win, load_sem.at[2])
    load_win.start()
    load_g.start()
    load_w.start()

    barrier = pltpu.get_barrier_semaphore()
    partners = [sibling]
    partners += [at(xs[i], y, z, k) for i in range(1, 4)]
    partners += [at(x, ys[i], z, k) for i in range(1, 8)]
    partners += [at(x, y, (z + i) % 8, k) for i in range(1, 8)]
    partners += [at(x, y, h * 4 + (c + i) % 4, 1 - k) for i in range(1, 4)]
    for partner in partners:
        pl.semaphore_signal(barrier, inc=1, device_id=partner, device_id_type=MESH)

    def slot(pz):
        return (pz % 4) * 2 + pz // 4

    def piece(b, j):
        return wt.at[b, pl.ds(16 * j, 16)]

    mine = slot(z)
    line = lax.broadcasted_iota(jnp.int32, (64, 128), 0)
    lane = lax.broadcasted_iota(jnp.int32, (64, 128), 1)
    pick = (line == lane).astype(F32).astype(BF16)
    load_win.wait()
    wt[mine] = lax.dot_general(
        pick, win[...], (((1,), (1,)), ((), ())), preferred_element_type=F32
    ).astype(BF16)
    pl.semaphore_wait(barrier, len(partners))

    to = (at(x, y, (z + 1) % 8, k), at(x, y, (z + 7) % 8, k))

    def ring(direction, b, step, j):
        return copy(
            piece(b, j), piece(b, j), ring_send,
            ring_recv.at[direction, step, j], to[direction],
        )

    for j in range(NQ):
        ring(0, mine, 0, j).start()
        ring(1, mine, 0, j).start()
    load_g.wait()
    copy(g.at[k], g.at[k], swap_send.at[0], swap_recv.at[0], sibling).start()
    load_w.wait()
    copy(w.at[k], w.at[k], swap_send.at[1], swap_recv.at[1], sibling).start()
    source = lax.broadcasted_iota(jnp.int32, (128, 256), 0)
    target = lax.broadcasted_iota(jnp.int32, (128, 256), 1)
    for pk in range(2):
        place[pk] = (target == (source // 8) * 16 + 8 * pk + source % 8).astype(F32).astype(BF16)
    for step in range(1, 4):
        for j in range(NQ):
            for direction in range(2):
                away = step if direction == 1 else 8 - step
                b = slot((z + away) % 8)
                arrived(piece(b, j), ring_recv.at[direction, step - 1, j])
                if step < 3 or direction == j // (NQ // 2):
                    ring(direction, b, step, j).start()
    far = slot((z + 4) % 8)
    for j in range(NQ):
        arrived(piece(far, j), ring_recv.at[j // (NQ // 2), 3, j])
    arrived(g.at[1 - k], swap_recv.at[0])

    def form(m):
        got = jnp.dot(
            wt[...].reshape(512, 1024), g[m // 2, :, 256 * (m % 2) : 256 * (m % 2) + 256],
            preferred_element_type=F32,
        )
        for u in range(U):
            for px in range(4):
                for py in range(8):
                    for ph in range(2):
                        a = 128 * px + 64 * ph + 8 * py
                        b = 16 * py + 8 * ph
                        pf[u, px, b : b + 8] = got[a : a + 8, CW * u : CW * u + CW]
        for u in range(U):
            n = U * m + u
            for away in (2, 1, 3):
                px = xs[away]
                part[n, away - 1] = pf[u, px].astype(BF16)
                copy(
                    part.at[n, away - 1], x_in.at[n, away - 1],
                    x_send, x_recv.at[n], at(px, y, z, k),
                ).start()
            own[n] = pf[u, x]

    def sum_x(n):
        arrived(x_in.at[n], x_recv.at[n])
        terms = x_in[n, 0].astype(F32) + x_in[n, 1].astype(F32) + x_in[n, 2].astype(F32)
        s[n] = (own[n] + terms).reshape(8, 16, CW)
        for away in (4, 3, 5, 2, 6, 1, 7):
            copy(
                s.at[n, ys[away]], y_in.at[n, away - 1],
                y_send, y_recv.at[n], at(x, ys[away], z, k),
            ).start()

    def spread(ph, n):
        for away in (4, 3, 5, 2, 6, 1, 7):
            copy(
                low.at[ph, n], gl.at[x, ph, n, y], ay_send,
                ay_recv.at[ph, n], at(x, ys[away], z, k),
            ).start()
        gl[x, ph, n, y] = low[ph, n]

    def sum_y(n):
        arrived(y_in.at[n], y_recv.at[n])
        total = s[n, y]
        for away in range(7):
            total += y_in[n, away]
        total = total * (1.0 / TOTAL)
        low[h, n] = total.astype(BF16)
        copy(low.at[h, n], low.at[h, n], low_send, low_recv.at[n], opposite).start()
        spread(h, n)
        t[n] = total
        copy(
            t.at[n, pl.ds(pl.multiple_of(8 * (1 - h), 8), 8)], gram_in.at[h, n],
            h_send, h_recv.at[n], opposite,
        ).start()
        gram_in[h, n] = t[n, pl.ds(pl.multiple_of(8 * h, 8), 8)]

    def spread_other(n):
        arrived(low.at[1 - h, n], low_recv.at[n])
        spread(1 - h, n)

    def pass_on(px, ph, n, send, recv, device):
        return copy(gl.at[px, ph, n], gl.at[px, ph, n], send, recv, device)

    def send_own(ph, n):
        arrived(gl.at[x, ph, n, pl.ds(0, 7)], ay_recv.at[ph, n])
        pass_on(x, ph, n, ax_send, ax_recv.at[0, ph, n], right).start()
        pass_on(x, ph, n, ax_send, ax_recv.at[1, ph, n], left).start()

    def send_near(ph, n):
        arrived(gl.at[xs[3], ph, n], ax_recv.at[0, ph, n])
        if n < CH // 2:
            pass_on(xs[3], ph, n, fw_send, ax_recv.at[2, ph, n], right).start()
        arrived(gl.at[xs[1], ph, n], ax_recv.at[1, ph, n])
        if n >= CH // 2:
            pass_on(xs[1], ph, n, fw_send, ax_recv.at[2, ph, n], left).start()

    def last(ph, n):
        arrived(gl.at[xs[2], ph, n], ax_recv.at[2, ph, n])

    def multiply(away, ph, n):
        if (n + 1) % U:
            return
        a = 1024 * ph + CW * (n + 1 - U)
        px = xs[away]
        low_rows = jnp.concatenate(
            [gl[px, ph, n + 1 - U + u].reshape(128, CW) for u in range(U)], axis=1
        )
        acc[away] += lax.dot_general(
            w[:, :, pl.ds(a, 256)].reshape(448, 256), low_rows,
            (((1,), (1,)), ((), ())), preferred_element_type=F32,
        )

    def give(away):
        px = xs[away]
        q[away] = acc[away].astype(BF16).reshape(2, 224, 128)
        for pk in range(2):
            here = (c == px) & (k == pk)

            @pl.when(here)
            def _():
                z_in[c, k] = q[away, pk]

            @pl.when(jnp.logical_not(here))
            def _():
                copy(
                    q.at[away, pk], z_in.at[c, k], z_send.at[away, pk], z_recv.at[c, k],
                    at(x, y, h * 4 + px, pk),
                ).start()

    def own_step(ph, n):
        send_own(ph, n)
        multiply(0, ph, n)

    def near_step(ph, n):
        send_near(ph, n)
        multiply(1, ph, n)
        multiply(3, ph, n)

    def last_step(ph, n):
        last(ph, n)
        multiply(2, ph, n)

    def run(stage, *args):
        if 0 <= args[-1] < CH:
            stage(*args)

    for m in range(CH // U):
        form(m)
    acc[...] = jnp.zeros_like(acc)
    arrived(w.at[1 - k], swap_recv.at[1])
    for n in range(CH + LAG_FAR2):
        run(sum_x, n)
        run(sum_y, n - LAG_Y)
        run(own_step, h, n - LAG_OWN)
        run(spread_other, n - LAG_H)
        run(own_step, 1 - h, n - LAG_OWN2)
        if n - LAG_OWN2 == CH - 1:
            give(0)
        run(near_step, h, n - LAG_NEAR)
        run(near_step, 1 - h, n - LAG_NEAR2)
        if n - LAG_NEAR2 == CH - 1:
            give(1)
            give(3)
        run(last_step, h, n - LAG_FAR)
        run(last_step, 1 - h, n - LAG_FAR2)
    give(2)

    for n in range(CH):
        arrived(gram_in.at[1 - h, n], h_recv.at[n])
    for ph in range(2):
        for n in range(CH):
            a = 1024 * ph + CW * n
            gram_ref[:, a : a + CW] = gram_in[ph, n]

    sent(wt.at[pl.ds(0, 7)], ring_send)
    sent(g.at[k], swap_send.at[0])
    sent(w.at[k], swap_send.at[1])
    sent(part, x_send)
    sent(y_in, y_send)
    sent(low.at[h], low_send)
    sent(gram_in.at[h], h_send)
    sent(gl.at[0, :, :, pl.ds(0, 7)], ay_send)
    sent(gl.at[pl.ds(0, 2)], ax_send)
    sent(gl.at[0], fw_send)

    for away in range(1, 4):
        for pk in range(2):
            pc = (c + away) % 4
            arrived(z_in.at[pc, pk], z_recv.at[pc, pk])
    arrived(z_in.at[c, 1 - k], z_recv.at[c, 1 - k])
    total = jnp.zeros((224, 256), F32)
    for pk in range(2):
        for pc in range(4):
            total += jnp.dot(z_in[pc, pk], place[pk], preferred_element_type=F32)
    prod_ref[...] = total

    for away in range(4):
        for pk in range(2):

            @pl.when(jnp.logical_not((c == (x + away) % 4) & (k == pk)))
            def _():
                sent(q.at[away, pk], z_send.at[away, pk])


def shards(grad_out, weight):
    dma = pltpu.SemaphoreType.DMA
    return pl.pallas_call(
        kernel,
        name="curvature",
        out_shape=(
            jax.ShapeDtypeStruct((8, 2048), F32),
            jax.ShapeDtypeStruct((224, 256), F32),
        ),
        in_specs=[pl.BlockSpec(memory_space=pltpu.HBM)] * 2,
        out_specs=(pl.BlockSpec(memory_space=pltpu.VMEM),) * 2,
        scratch_shapes=[
            pltpu.VMEM((1024, 128), BF16),
            pltpu.VMEM((2, 1024, 512), BF16),
            pltpu.VMEM((8, 64, 1024), BF16),
            pltpu.VMEM((2, 128, 256), BF16),
            pltpu.VMEM((U, 4, 128, CW), F32),
            pltpu.VMEM((CH, 3, 128, CW), BF16),
            pltpu.VMEM((CH, 128, CW), F32),
            pltpu.VMEM((CH, 3, 128, CW), BF16),
            pltpu.VMEM((CH, 8, 16, CW), F32),
            pltpu.VMEM((CH, 7, 16, CW), F32),
            pltpu.VMEM((CH, 16, CW), F32),
            pltpu.VMEM((2, CH, 8, CW), F32),
            pltpu.VMEM((2, CH, 16, CW), BF16),
            pltpu.VMEM((2, 224, 2048), BF16),
            pltpu.VMEM((4, 2, CH, 8, 16, CW), BF16),
            pltpu.VMEM((4, 448, 128), F32),
            pltpu.VMEM((4, 2, 224, 128), BF16),
            pltpu.VMEM((4, 2, 224, 128), BF16),
            dma((3,)),
            dma((2,)), dma((2,)),
            dma, dma((2, 4, NQ)),
            dma, dma((CH,)),
            dma, dma((CH,)),
            dma, dma((CH,)),
            dma, dma((CH,)),
            dma, dma((2, CH)),
            dma, dma((3, 2, CH)), dma,
            dma((4, 2)), dma((4, 2)),
        ],
        compiler_params=pltpu.CompilerParams(
            collective_id=0, has_side_effects=True, vmem_limit_bytes=53 * 2**20
        ),
        cost_estimate=pl.CostEstimate(flops=2 * 10**9, bytes_accessed=3 * 2**20, transcendentals=0),
    )(grad_out, weight)


def solution(mesh):
    placed = (P("dp", ("col", "row")), P(("dp", "row"), "col"))
    return jax.shard_map(
        shards,
        mesh=mesh,
        in_specs=placed,
        out_specs=(P(("dp", "row"), "col"), P(("dp", "row"), "col")),
        check_vma=False,
    )
```

time: 85.1 us -> 79.4 us (0.933)
  Pallas kernels: 80.5 us -> 77.3 us
  local copies, waits for them, and re-layouts: 3.72 us -> 1.32 us
    pallas_call x1, Pallas kernels: 80.5 us -> 77.3 us  [shards(): pl.pallas_call(kernel, name='curvature', out_shape=(jax.ShapeDtypeStruct(...]
    unnamed x6 -> x2, local copies, waits for them, and re-layouts: 3.72 us -> 1.32 us
where the time goes in v3:
time: 79.4 us; the launch traced here: 79.2 us
  Pallas kernels  77.3 us (97%)
  local copies, waits for them, and re-layouts  1.32 us (2%)
    pallas_call x1, Pallas kernels, shards(): pl.pallas_call(kernel, name='curvature', out_shape=(jax.ShapeDtypeStruct(...  77.3 us

profile of v3, /device:TPU:5, one launch (start us, length us, event | category | flops | bytes accessed | tf_op | source)
XLA Modules:
  0.0 79.2 jit_solution(9832837660449027458)
XLA Ops:
  0.6 77.3 %curvature.1 = (f32[8,2048]{1,0:T(8,128)S(1)}, f32[224,256]{1,0:T(8,128)S(1)}) custom-call(bf16[1024,512]{1,0:T(8,128)(2,1)} %g_hbm.1, bf16[224,2048]{1,0:T(8,128)(2,1)} %w_hbm.1), custom_call_target="tpu_custom_call" | custom-call | flops 2000000000 | bytes 3145728 | tf_op jit(solution)/shard_map/curvature/pallas_call | solution.py:302
  77.9 0.6 copy.6
  78.5 0.7 copy.7

commit v4 on v3

--- a/solution.py
+++ b/solution.py
@@ -8,11 +8,12 @@
 MESH = pl.DeviceIdType.MESH
 F32, BF16 = jnp.float32, jnp.bfloat16
 TOTAL = 32768
-CH = 4
-CW = 1024 // CH
-U = 256 // CW
+CW = 128
+CH = 8
+PARTS = ((0, 2), (2, 2), (4, 2), (6, 2))
+NP = len(PARTS)
 NQ = 4
-LAG_Y, LAG_OWN, LAG_H, LAG_OWN2, LAG_NEAR, LAG_NEAR2, LAG_FAR, LAG_FAR2 = 1, 2, 2, 3, 3, 4, 4, 5
+LAG_Y, LAG_OWN, LAG_H, LAG_OWN2, LAG_NEAR, LAG_NEAR2, LAG_FAR, LAG_FAR2 = 1, 2, 2, 3, 3, 4, 5, 5
 
 
 def kernel(
@@ -117,93 +118,105 @@
             wt[...].reshape(512, 1024), g[m // 2, :, 256 * (m % 2) : 256 * (m % 2) + 256],
             preferred_element_type=F32,
         )
-        for u in range(U):
+        for u in range(2):
             for px in range(4):
                 for py in range(8):
                     for ph in range(2):
                         a = 128 * px + 64 * ph + 8 * py
                         b = 16 * py + 8 * ph
                         pf[u, px, b : b + 8] = got[a : a + 8, CW * u : CW * u + CW]
-        for u in range(U):
-            n = U * m + u
+        for i in range(2):
             for away in (2, 1, 3):
-                px = xs[away]
-                part[n, away - 1] = pf[u, px].astype(BF16)
-                copy(
-                    part.at[n, away - 1], x_in.at[n, away - 1],
-                    x_send, x_recv.at[n], at(px, y, z, k),
-                ).start()
-            own[n] = pf[u, x]
-
-    def sum_x(n):
-        arrived(x_in.at[n], x_recv.at[n])
-        terms = x_in[n, 0].astype(F32) + x_in[n, 1].astype(F32) + x_in[n, 2].astype(F32)
-        s[n] = (own[n] + terms).reshape(8, 16, CW)
+                part[2 * m + i, away - 1] = pf[i, xs[away]].astype(BF16)
+            own[2 * m + i] = pf[i, x]
+        for p, (n, units) in enumerate(PARTS):
+            if (n + units - 1) // 2 == m:
+                here = pl.ds(n, units)
+                for away in (2, 1, 3):
+                    copy(
+                        part.at[here, away - 1], x_in.at[here, away - 1],
+                        x_send, x_recv.at[p], at(xs[away], y, z, k),
+                    ).start()
+
+    def sum_x(p):
+        first, units = PARTS[p]
+        here = pl.ds(first, units)
+        arrived(x_in.at[here], x_recv.at[p])
+        for n in range(first, first + units):
+            terms = x_in[n, 0].astype(F32) + x_in[n, 1].astype(F32) + x_in[n, 2].astype(F32)
+            s[n] = (own[n] + terms).reshape(8, 16, CW)
         for away in (4, 3, 5, 2, 6, 1, 7):
             copy(
-                s.at[n, ys[away]], y_in.at[n, away - 1],
-                y_send, y_recv.at[n], at(x, ys[away], z, k),
+                s.at[here, ys[away]], y_in.at[here, away - 1], y_send, y_recv.at[p],
+                at(x, ys[away], z, k),
             ).start()
 
-    def spread(ph, n):
+    def spread(ph, p):
+        here = pl.ds(*PARTS[p])
         for away in (4, 3, 5, 2, 6, 1, 7):
             copy(
-                low.at[ph, n], gl.at[x, ph, n, y], ay_send,
-                ay_recv.at[ph, n], at(x, ys[away], z, k),
+                low.at[ph, here], gl.at[x, ph, here, y], ay_send, ay_recv.at[ph, p],
+                at(x, ys[away], z, k),
             ).start()
-        gl[x, ph, n, y] = low[ph, n]
-
-    def sum_y(n):
-        arrived(y_in.at[n], y_recv.at[n])
-        total = s[n, y]
-        for away in range(7):
-            total += y_in[n, away]
-        total = total * (1.0 / TOTAL)
-        low[h, n] = total.astype(BF16)
-        copy(low.at[h, n], low.at[h, n], low_send, low_recv.at[n], opposite).start()
-        spread(h, n)
-        t[n] = total
+        for n in range(PARTS[p][0], sum(PARTS[p])):
+            gl[x, ph, n, y] = low[ph, n]
+
+    def sum_y(p):
+        first, units = PARTS[p]
+        here = pl.ds(first, units)
+        arrived(y_in.at[here], y_recv.at[p])
+        for n in range(first, first + units):
+            total = s[n, y]
+            for away in range(7):
+                total += y_in[n, away]
+            total = total * (1.0 / TOTAL)
+            low[h, n] = total.astype(BF16)
+            t[n] = total
+        copy(low.at[h, here], low.at[h, here], low_send, low_recv.at[p], opposite).start()
+        spread(h, p)
         copy(
-            t.at[n, pl.ds(pl.multiple_of(8 * (1 - h), 8), 8)], gram_in.at[h, n],
-            h_send, h_recv.at[n], opposite,
+            t.at[here, pl.ds(pl.multiple_of(8 * (1 - h), 8), 8)], gram_in.at[h, here],
+            h_send, h_recv.at[p], opposite,
         ).start()
-        gram_in[h, n] = t[n, pl.ds(pl.multiple_of(8 * h, 8), 8)]
-
-    def spread_other(n):
-        arrived(low.at[1 - h, n], low_recv.at[n])
-        spread(1 - h, n)
-
-    def pass_on(px, ph, n, send, recv, device):
-        return copy(gl.at[px, ph, n], gl.at[px, ph, n], send, recv, device)
-
-    def send_own(ph, n):
-        arrived(gl.at[x, ph, n, pl.ds(0, 7)], ay_recv.at[ph, n])
-        pass_on(x, ph, n, ax_send, ax_recv.at[0, ph, n], right).start()
-        pass_on(x, ph, n, ax_send, ax_recv.at[1, ph, n], left).start()
-
-    def send_near(ph, n):
-        arrived(gl.at[xs[3], ph, n], ax_recv.at[0, ph, n])
-        if n < CH // 2:
-            pass_on(xs[3], ph, n, fw_send, ax_recv.at[2, ph, n], right).start()
-        arrived(gl.at[xs[1], ph, n], ax_recv.at[1, ph, n])
-        if n >= CH // 2:
-            pass_on(xs[1], ph, n, fw_send, ax_recv.at[2, ph, n], left).start()
-
-    def last(ph, n):
-        arrived(gl.at[xs[2], ph, n], ax_recv.at[2, ph, n])
-
-    def multiply(away, ph, n):
-        if (n + 1) % U:
-            return
-        a = 1024 * ph + CW * (n + 1 - U)
+        for n in range(first, first + units):
+            gram_in[h, n] = t[n, pl.ds(pl.multiple_of(8 * h, 8), 8)]
+
+    def spread_other(p):
+        arrived(low.at[1 - h, pl.ds(*PARTS[p])], low_recv.at[p])
+        spread(1 - h, p)
+
+    def pass_on(px, ph, p, send, recv, device):
+        here = pl.ds(*PARTS[p])
+        return copy(gl.at[px, ph, here], gl.at[px, ph, here], send, recv, device)
+
+    def send_own(ph, p):
+        arrived(gl.at[x, ph, pl.ds(*PARTS[p]), pl.ds(0, 7)], ay_recv.at[ph, p])
+        pass_on(x, ph, p, ax_send, ax_recv.at[0, ph, p], right).start()
+        pass_on(x, ph, p, ax_send, ax_recv.at[1, ph, p], left).start()
+
+    def send_near(ph, p, other):
+        here = pl.ds(*PARTS[p])
+        arrived(gl.at[xs[3], ph, here], ax_recv.at[0, ph, p])
+        if not other:
+            pass_on(xs[3], ph, p, fw_send, ax_recv.at[2, ph, p], right).start()
+        arrived(gl.at[xs[1], ph, here], ax_recv.at[1, ph, p])
+        if other:
+            pass_on(xs[1], ph, p, fw_send, ax_recv.at[2, ph, p], left).start()
+
+    def last(ph, p):
+        arrived(gl.at[xs[2], ph, pl.ds(*PARTS[p])], ax_recv.at[2, ph, p])
+
+    def multiply(away, ph, p):
         px = xs[away]
-        low_rows = jnp.concatenate(
-            [gl[px, ph, n + 1 - U + u].reshape(128, CW) for u in range(U)], axis=1
-        )
-        acc[away] += lax.dot_general(
-            w[:, :, pl.ds(a, 256)].reshape(448, 256), low_rows,
-            (((1,), (1,)), ((), ())), preferred_element_type=F32,
-        )
+        for n in range(PARTS[p][0] // 2 * 2, sum(PARTS[p]) // 2 * 2, 2):
+            a = 1024 * ph + CW * n
+            low_rows = jnp.concatenate(
+                [gl[px, ph, n].reshape(128, CW), gl[px, ph, n + 1].reshape(128, CW)], axis=1
+            )
+            acc[away] += lax.dot_general(
+                w[:, :, pl.ds(a, 256)].reshape(448, 256), low_rows,
+                (((1,), (1,)), ((), ())), preferred_element_type=F32,
+            )
 
     def give(away):
         px = xs[away]
@@ -222,46 +235,41 @@
                     at(x, y, h * 4 + px, pk),
                 ).start()
 
-    def own_step(ph, n):
-        send_own(ph, n)
-        multiply(0, ph, n)
-
-    def near_step(ph, n):
-        send_near(ph, n)
-        multiply(1, ph, n)
-        multiply(3, ph, n)
-
-    def last_step(ph, n):
-        last(ph, n)
-        multiply(2, ph, n)
-
-    def run(stage, *args):
-        if 0 <= args[-1] < CH:
-            stage(*args)
-
-    for m in range(CH // U):
+    def run(stage, p, *args):
+        if 0 <= p < NP:
+            stage(p, *args)
+
+    for m in range(CH // 2):
         form(m)
     acc[...] = jnp.zeros_like(acc)
     arrived(w.at[1 - k], swap_recv.at[1])
-    for n in range(CH + LAG_FAR2):
-        run(sum_x, n)
-        run(sum_y, n - LAG_Y)
-        run(own_step, h, n - LAG_OWN)
-        run(spread_other, n - LAG_H)
-        run(own_step, 1 - h, n - LAG_OWN2)
-        if n - LAG_OWN2 == CH - 1:
+    for p in range(NP + LAG_FAR2):
+        run(sum_x, p)
+        run(sum_y, p - LAG_Y)
+        run(spread_other, p - LAG_H)
+        run(lambda q: send_own(h, q), p - LAG_OWN)
+        run(lambda q: send_near(h, q, False), p - LAG_NEAR)
+        run(lambda q: send_own(1 - h, q), p - LAG_OWN2)
+        run(lambda q: send_near(1 - h, q, True), p - LAG_NEAR2)
+        run(lambda q: multiply(0, h, q), p - LAG_OWN)
+        run(lambda q: multiply(0, 1 - h, q), p - LAG_OWN2)
+        if p - LAG_OWN2 == NP - 1:
             give(0)
-        run(near_step, h, n - LAG_NEAR)
-        run(near_step, 1 - h, n - LAG_NEAR2)
-        if n - LAG_NEAR2 == CH - 1:
+        run(lambda q: multiply(1, h, q), p - LAG_NEAR)
+        run(lambda q: multiply(3, h, q), p - LAG_NEAR)
+        run(lambda q: multiply(1, 1 - h, q), p - LAG_NEAR2)
+        run(lambda q: multiply(3, 1 - h, q), p - LAG_NEAR2)
+        if p - LAG_NEAR2 == NP - 1:
             give(1)
             give(3)
-        run(last_step, h, n - LAG_FAR)
-        run(last_step, 1 - h, n - LAG_FAR2)
+        run(lambda q: last(h, q), p - LAG_FAR)
+        run(lambda q: multiply(2, h, q), p - LAG_FAR)
+        run(lambda q: last(1 - h, q), p - LAG_FAR2)
+        run(lambda q: multiply(2, 1 - h, q), p - LAG_FAR2)
     give(2)
 
-    for n in range(CH):
-        arrived(gram_in.at[1 - h, n], h_recv.at[n])
+    for p in range(NP):
+        arrived(gram_in.at[1 - h, pl.ds(*PARTS[p])], h_recv.at[p])
     for ph in range(2):
         for n in range(CH):
             a = 1024 * ph + CW * n
@@ -313,7 +321,7 @@
             pltpu.VMEM((2, 1024, 512), BF16),
             pltpu.VMEM((8, 64, 1024), BF16),
             pltpu.VMEM((2, 128, 256), BF16),
-            pltpu.VMEM((U, 4, 128, CW), F32),
+            pltpu.VMEM((2, 4, 128, CW), F32),
             pltpu.VMEM((CH, 3, 128, CW), BF16),
             pltpu.VMEM((CH, 128, CW), F32),
             pltpu.VMEM((CH, 3, 128, CW), BF16),
@@ -330,12 +338,12 @@
             dma((3,)),
             dma((2,)), dma((2,)),
             dma, dma((2, 4, NQ)),
-            dma, dma((CH,)),
-            dma, dma((CH,)),
-            dma, dma((CH,)),
-            dma, dma((CH,)),
-            dma, dma((2, CH)),
-            dma, dma((3, 2, CH)), dma,
+            dma, dma((NP,)),
+            dma, dma((NP,)),
+            dma, dma((NP,)),
+            dma, dma((NP,)),
+            dma, dma((2, NP)),
+            dma, dma((3, 2, NP)), dma,
             dma((4, 2)), dma((4, 2)),
         ],
         compiler_params=pltpu.CompilerParams(

time: 79.4 us -> 78.9 us (level)
  no operation moved by 1% of the time
where the time goes in v4:
time: 78.9 us; the launch traced here: 78.7 us
  Pallas kernels  76.8 us (97%)
  local copies, waits for them, and re-layouts  1.32 us (2%)
    pallas_call x1, Pallas kernels, shards(): pl.pallas_call(kernel, name='curvature', out_shape=(jax.ShapeDtypeStruct(...  76.8 us

profile of v4, /device:TPU:5, one launch (start us, length us, event | category | flops | bytes accessed | tf_op | source)
XLA Modules:
  0.0 78.7 jit_solution(16768275760671981644)
XLA Ops:
  0.6 76.8 %curvature.1 = (f32[8,2048]{1,0:T(8,128)S(1)}, f32[224,256]{1,0:T(8,128)S(1)}) custom-call(bf16[1024,512]{1,0:T(8,128)(2,1)} %g_hbm.1, bf16[224,2048]{1,0:T(8,128)(2,1)} %w_hbm.1), custom_call_target="tpu_custom_call" | custom-call | flops 2000000000 | bytes 3145728 | tf_op jit(solution)/shard_map/curvature/pallas_call | solution.py:310
  77.4 0.6 copy.6
  78.1 0.7 copy.7
